TPU v7x, 32 devices: a whole 2x2x4 slice. The times are simulated.
32 devices in a mesh: row: 8 (over z, x), col: 4 (over y, core).
Axes of the slice: x: 2, y: 2, z: 4, core: 2. Of those that a mesh axis runs over, the one named last changes fastest.
Arguments:
- query_grads: bfloat16 [27648, 256], P(('row', 'col')), may hold values from -6 to 6
- eigenbasis: bfloat16 [27648, 27648], P('row', 'col'), may hold values from -0.0546875 to 0.0546875
- eigenvalues: float32 [27648], P('col'), may hold values from 0.05 to 20
- activations: bfloat16 [1024, 8, 3456], P('row', None, 'col'), may hold values from -0.0390625 to 0.0390625
Outputs:
- scores: float32 [256, 1024], P('col', 'row')
All inputs are finite; a program needn't handle non-finite values.
Results may differ from a plain program's by a relative error of at most 0.0037.
Values may be sent and summed in bfloat16 or wider, within the bound.
A program may use at most 128 MiB of HBM per device.

v0:
```python
import jax
import jax.numpy as jnp
from jax import lax
from jax.sharding import PartitionSpec as P


def filter_weights(values):
    return (1.0 - jnp.exp(-values)) / values


def local(query_grads, eigenbasis, eigenvalues, activations):
    grad_block = lax.all_gather(query_grads, "col", axis=0, tiled=True)
    share = eigenbasis.shape[1] // lax.axis_size("row")
    partial_rot = lax.psum_scatter(
        lax.dot_general(
            eigenbasis, grad_block, (((0,), (0,)), ((), ())), preferred_element_type=jnp.float32
        ),
        "row",
        scatter_dimension=0,
        tiled=True,
    )
    local_vals = lax.dynamic_slice_in_dim(eigenvalues, lax.axis_index("row") * share, share, 0)
    filtered = (partial_rot * filter_weights(local_vals)[:, None]).astype(jnp.bfloat16)
    whole_cols = lax.all_gather(filtered, "row", axis=0, tiled=True)
    restored = lax.psum_scatter(
        jnp.dot(eigenbasis, whole_cols, preferred_element_type=jnp.float32),
        "col",
        scatter_dimension=0,
        tiled=True,
    ).astype(jnp.bfloat16)
    blocks = lax.all_gather(restored, "row", axis=0, tiled=True)
    flat = activations.reshape(activations.shape[0], -1)
    return lax.psum_scatter(
        lax.dot_general(blocks, flat, (((0,), (1,)), ((), ())), preferred_element_type=jnp.float32),
        "col",
        scatter_dimension=0,
        tiled=True,
    )


def solution(mesh):
    in_specs = (P(("row", "col"), None), P("row", "col"), P("col"), P("row", None, "col"))
    out_specs = P("col", "row")
    return jax.shard_map(local, mesh=mesh, in_specs=in_specs, out_specs=out_specs, check_vma=False)
```

profile of v0, /device:TPU:0, one launch (start us, length us, event | category | flops | bytes accessed | tf_op | source)
XLA Modules:
  0.0 415.5 jit_solution(8214557480739194404)
XLA Ops:
  6.5 0.0 copy-start
  6.5 0.0 all-gather.4.cloned.1.call-start
  6.5 0.7 all-gather.4.cloned.1.call-update
  7.3 0.0 reduce-scatter.6.cloned.1.call-start
  7.3 25.1 %all-gather.4.cloned.1.call-done = bf16[3456,256]{1,0:T(8,128)(2,1)} async-done(((bf16[864,256]{1,0:T(8,128)(2,1)}), bf16[3456,256]{1,0:T(8,128)(2,1)}) %all-gather.4.cloned.1.call-update) | async-done | bytes 1769488 | tf_op jit(solution)/shard_map/all_gather | solution.py:12
  32.4 23.8 %fusion = f32[6912,256]{1,0:T(8,128)} fusion(bf16[3456,6912]{1,0:T(8,128)(2,1)} %param.5, bf16[3456,256]{1,0:T(8,128)(2,1)} %all-gather.4.cloned.1.call-done), kind=kOutput, calls=%fused_computation.3 | convolution fusion | flops 12230590464 | bytes 56623104 | tf_op jit(solution)/shard_map/dot_general | solution.py:15
  56.2 0.0 reduce-scatter.6.cloned.1.call-update
  56.2 0.0 all-gather.6.cloned.1.call-start
  56.3 0.8 subtract_divide_fusion
  57.1 128.3 %reduce-scatter.6.cloned.1.call-done = f32[864,256]{1,0:T(8,128)} async-done(((f32[6912,256]{1,0:T(8,128)}), f32[864,256]{1,0:T(8,128)}) %reduce-scatter.6.cloned.1.call-update) | async-done | bytes 884752 | tf_op jit(solution)/shard_map/reduce_scatter | solution.py:14
  185.4 2.1 multiply_convert_fusion
  187.5 0.0 all-gather.6.cloned.1.call-update
  187.5 0.0 reduce-scatter.10.cloned.1.call-start
  187.6 64.5 %all-gather.6.cloned.1.call-done = bf16[6912,256]{1,0:T(8,128)(2,1)} async-done(((bf16[864,256]{1,0:T(8,128)(2,1)}), bf16[6912,256]{1,0:T(8,128)(2,1)}) %all-gather.6.cloned.1.call-update) | async-done | bytes 3538960 | tf_op jit(solution)/shard_map/all_gather | solution.py:24
  252.1 23.0 %convolution_bitcast_fusion = f32[3456,256]{0,1:T(8,128)} fusion(bf16[6912,256]{1,0:T(8,128)(2,1)} %all-gather.6.cloned.1.call-done, bf16[3456,6912]{1,0:T(8,128)(2,1)} %param.5), kind=kOutput, calls=%fused_computation | convolution fusion | flops 12230590464 | bytes 54853632 | tf_op jit(solution)/shard_map/dot_general | solution.py:26
  275.1 5.2 %copy.7 = f32[3456,256]{1,0:T(8,128)} copy(f32[3456,256]{0,1:T(8,128)} %convolution_bitcast_fusion) | data formatting | bytes 7077888
  280.2 0.0 reduce-scatter.10.cloned.1.call-update
  280.2 0.0 all-gather.8.cloned.1.call-start
  280.3 39.0 %reduce-scatter.10.cloned.1.call-done = f32[864,256]{1,0:T(8,128)} async-done(((f32[3456,256]{1,0:T(8,128)}), f32[864,256]{1,0:T(8,128)}) %reduce-scatter.10.cloned.1.call-update) | async-done | bytes 884752 | tf_op jit(solution)/shard_map/reduce_scatter | solution.py:25
  319.3 2.0 convert_element_type.7
  321.3 0.0 all-gather.8.cloned.1.call-update
  321.3 0.0 reduce-scatter.8.cloned.1.call-start
  321.4 65.3 %all-gather.8.cloned.1.call-done = bf16[6912,256]{1,0:T(8,128)(2,1)} async-done(((bf16[864,256]{1,0:T(8,128)(2,1)}), bf16[6912,256]{1,0:T(8,128)(2,1)}) %all-gather.8.cloned.1.call-update) | async-done | bytes 3538960 | tf_op jit(solution)/shard_map/all_gather | solution.py:31
  386.7 0.0 copy-done
  386.7 3.8 fusion.1
  390.4 0.0 reduce-scatter.8.cloned.1.call-update
  390.5 18.2 %reduce-scatter.8.cloned.1.call-done = f32[64,128]{1,0:T(8,128)} async-done(((f32[256,128]{1,0:T(8,128)}), f32[64,128]{1,0:T(8,128)}) %reduce-scatter.8.cloned.1.call-update) | async-done | bytes 32784 | tf_op jit(solution)/shard_map/reduce_scatter | solution.py:33
Async XLA Ops:
  6.5 380.1 %copy-start = (bf16[128,8,864]{0,2,1:T(8,128)(2,1)S(1)}, bf16[128,8,864]{0,2,1:T(8,128)(2,1)}, u32[]{:S(2)}) copy-start(bf16[128,8,864]{0,2,1:T(8,128)(2,1)} %param.7) | copy-start | bytes 5308420
  6.5 25.9 %all-gather.4.cloned.1.call-start = ((), (), s32[]{:S(2)}) async-start(), calls=%async_computation.3 | async-start | bytes 2211840 | tf_op jit(solution)/shard_map/all_gather | solution.py:12
  7.3 178.1 %reduce-scatter.6.cloned.1.call-start = ((), (), s32[]{:S(2)}) async-start(), calls=%async_computation.4 | async-start | bytes 7962624 | tf_op jit(solution)/shard_map/reduce_scatter | solution.py:14
  56.2 195.8 %all-gather.6.cloned.1.call-start = ((), (), s32[]{:S(2)}) async-start(), calls=%async_computation.5 | async-start | bytes 3981312 | tf_op jit(solution)/shard_map/all_gather | solution.py:24
  187.5 131.8 %reduce-scatter.10.cloned.1.call-start = ((), (), s32[]{:S(2)}) async-start(), calls=%async_computation.8 | async-start | bytes 4423680 | tf_op jit(solution)/shard_map/reduce_scatter | solution.py:25
  280.2 106.4 %all-gather.8.cloned.1.call-start = ((), (), s32[]{:S(2)}) async-start(), calls=%async_computation.6 | async-start | bytes 3981312 | tf_op jit(solution)/shard_map/all_gather | solution.py:31
  321.3 87.4 %reduce-scatter.8.cloned.1.call-start = ((), (), s32[]{:S(2)}) async-start(), calls=%async_computation.7 | async-start | bytes 163840 | tf_op jit(solution)/shard_map/reduce_scatter | solution.py:33
Sparse Core Ops, SparseCore 0:
  8.9 23.4 all-gather.3
  56.4 128.9 reduce-scatter.5
  187.8 64.2 all-gather.5
  280.4 38.8 reduce-scatter.9
  321.4 65.1 all-gather.7
  390.6 18.0 reduce-scatter.7
where the time goes:
time: 416 us
  waiting for transfers between devices  341 us (82%)
  matrix products  50.6 us (12%)
  between operations  13.5 us (3%)
  local copies, waits for them, and re-layouts  5.18 us (1%)
  other arithmetic  4.88 us (1%)
    reduce_scatter x1, waiting for transfers between devices, local(): lax.psum_scatter(lax.dot_general(eigenbasis, grad_block, (((0,), (0,)), (...  128 us
    all_gather x1, waiting for transfers between devices, local(): blocks = lax.all_gather(restored, 'row', axis=0, tiled=True)  65.3 us
    all_gather x1, waiting for transfers between devices, local(): whole_cols = lax.all_gather(filtered, 'row', axis=0, tiled=True)  64.5 us
    reduce_scatter x1, waiting for transfers between devices, local(): lax.psum_scatter(jnp.dot(eigenbasis, whole_cols, preferred_element_type=j...  39 us
    all_gather x1, waiting for transfers between devices, local(): grad_block = lax.all_gather(query_grads, 'col', axis=0, tiled=True)  25.1 us
    dot_general x1, matrix products, local(): lax.dot_general(eigenbasis, grad_block, (((0,), (0,)), ((), ())), preferr...  23.8 us
    dot_general x1, matrix products, local(): jnp.dot(eigenbasis, whole_cols, preferred_element_type=jnp.float32)  23 us
    reduce_scatter x1, waiting for transfers between devices, local(): lax.psum_scatter(lax.dot_general(blocks, flat, (((0,), (1,)), ((), ())),...  18.2 us
  transfers between devices with their start and end apart: 6, of which 6 were waited for; matrix products, arithmetic and copies ran while one was open for 0% of the time, Pallas kernels for 0%

commit v1 on v0

--- a/solution.py
+++ b/solution.py
@@ -1,14 +1,309 @@
+import functools
+
 import jax
 import jax.numpy as jnp
 from jax import lax
+from jax.experimental import pallas as pl
+from jax.experimental.pallas import tpu as pltpu
 from jax.sharding import PartitionSpec as P
+
+CHUNKS = 9
+LAG = 6
+F32, BF16 = jnp.float32, jnp.bfloat16
+NT = (((1,), (1,)), ((), ()))
 
 
 def filter_weights(values):
     return (1.0 - jnp.exp(-values)) / values
 
 
-def local(query_grads, eigenbasis, eigenvalues, activations):
+def kernel(
+    gt_ref, u_ref, w_ref, act_ref, out_ref,
+    gt, u1, u2, part, send, recv, filt, rest, core_in, y_out, y_in,
+    acts, tot, tot_core, tot_y, tot_row,
+    u1_sem, u2_sem, g_send, g_recv, a_send, a_recv, a_own, x_send, x_recv,
+    r_send, r_recv, t_send, t_recv,
+):
+    row, col = lax.axis_index("row"), lax.axis_index("col")
+    b0, b1, b2 = lax.rem(row, 2), lax.rem(lax.div(row, 2), 2), lax.div(row, 4)
+    core, y = lax.rem(col, 2), lax.div(col, 2)
+    peers = (row + 1 - 2 * b0, row + 2 - 4 * b1, row + 4 - 8 * b2)
+    core_peer, y_peer = col + 1 - 2 * core, col + 2 - 4 * y
+    mc = u1.shape[2]
+    depth = gt.shape[2]
+
+    def copy(src, dst, ssem, rsem, r, c):
+        return pltpu.make_async_remote_copy(
+            src_ref=src, dst_ref=dst, send_sem=ssem, recv_sem=rsem,
+            device_id=(r, c), device_id_type=pl.DeviceIdType.MESH,
+        )
+
+    def load(c, buf, sem):
+        slot = lax.rem(c, 2)
+        cols = pl.ds(pl.multiple_of(c * mc, 128), mc)
+        return pltpu.make_async_copy(u_ref.at[:, cols], buf.at[slot], sem.at[slot])
+
+    load(0, u1, u1_sem).start()
+
+    barrier = pltpu.get_barrier_semaphore()
+    for d in range(1, 8):
+        pl.semaphore_signal(barrier, inc=1, device_id=(lax.rem(row + d, 8), col),
+                            device_id_type=pl.DeviceIdType.MESH)
+    for c in (core_peer, y_peer):
+        pl.semaphore_signal(barrier, inc=1, device_id=(row, c),
+                            device_id_type=pl.DeviceIdType.MESH)
+    pl.semaphore_wait(barrier, 9)
+
+    own_y = copy(gt_ref, gt.at[col], g_send.at[0], g_recv.at[0], row, y_peer)
+    own_c = copy(gt_ref, gt.at[col], g_send.at[1], g_recv.at[1], row, core_peer)
+    own_y.start()
+    own_c.start()
+    gt[col] = gt_ref[...]
+
+    own_a = pltpu.make_async_copy(act_ref.at[row], acts.at[row], a_own)
+    own_a.start()
+
+    def act_copy(d):
+        to = lax.rem(row + d, 8)
+        return copy(act_ref.at[to], acts.at[row], a_send.at[d], a_recv.at[d], to, col)
+
+    def act_arrival(d):
+        origin = lax.rem(row + 8 - d, 8)
+        return copy(act_ref.at[row], acts.at[origin], a_send.at[d], a_recv.at[d], origin, col)
+
+    for d in range(1, 8):
+        act_copy(d).start()
+
+    rest[...] = jnp.zeros_like(rest)
+
+    copy(gt_ref, gt.at[y_peer], g_send.at[0], g_recv.at[0], row, y_peer).wait_recv()
+    fwd = copy(gt.at[y_peer], gt.at[y_peer], g_send.at[2], g_recv.at[2], row, core_peer)
+    fwd.start()
+    copy(gt_ref, gt.at[core_peer], g_send.at[1], g_recv.at[1], row, core_peer).wait_recv()
+    diagonal = (1 - y) * 2 + 1 - core
+    copy(gt.at[y_peer], gt.at[diagonal], g_send.at[2], g_recv.at[2], row, core_peer).wait_recv()
+
+    def rows(start, size):
+        return pl.ds(pl.multiple_of(start, 32), size)
+
+    keep = (rows(128 * b0, 128), rows(128 * b0 + 64 * b1, 64), rows(128 * b0 + 64 * b1 + 32 * b2, 32))
+    give = (
+        rows(128 * (1 - b0), 128),
+        rows(128 * b0 + 64 * (1 - b1), 64),
+        rows(128 * b0 + 64 * b1 + 32 * (1 - b2), 32),
+    )
+    slab = (pl.ds(0, 128), pl.ds(128, 64), pl.ds(192, 32))
+
+    def halving(c, k):
+        return copy(send.at[c, slab[k]], recv.at[c, slab[k]], x_send.at[k, c], x_recv.at[k, c],
+                    peers[k], col)
+
+    def doubling(c, k):
+        return copy(filt.at[c, keep[k]], filt.at[c, keep[k]], x_send.at[3 + k, c],
+                    x_recv.at[3 + k, c], peers[k], col)
+
+    def doubled(c, k):
+        return copy(filt.at[c, give[k]], filt.at[c, give[k]], x_send.at[3 + k, c],
+                    x_recv.at[3 + k, c], peers[k], col)
+
+    def hand_on(c, k):
+        send[c, slab[k]] = part[c, give[k]].astype(BF16)
+        halving(c, k).start()
+
+    def stage(s, lag, body):
+        c = s - lag
+        pl.when(jnp.logical_and(c >= 0, c < CHUNKS))(lambda: body(c))
+
+    def gathered(c):
+        doubled(c, 1).wait_recv()
+        doubling(c, 0).start()
+
+    def gather(c):
+        doubled(c, 2).wait_recv()
+        doubling(c, 1).start()
+
+    def scale(c):
+        halving(c, 2).wait_recv()
+        total = part[c, keep[2]] + recv[c, slab[2]].astype(F32)
+        filt[c, keep[2]] = (total * w_ref[c]).astype(BF16)
+        doubling(c, 2).start()
+
+    def add(k):
+        def body(c):
+            halving(c, k).wait_recv()
+            part[c, keep[k]] += recv[c, slab[k]].astype(F32)
+            hand_on(c, k + 1)
+        return body
+
+    def rotate(c):
+        slot = lax.rem(c, 2)
+        load(c, u1, u1_sem).wait()
+        pl.when(c + 1 < CHUNKS)(lambda: load(c + 1, u1, u1_sem).start())
+
+        def tile(t, carry):
+            cols = pl.ds(pl.multiple_of(t * 256, 256), 256)
+            total = jnp.zeros((256, 256), F32)
+            for j in range(4):
+                total += jnp.dot(gt[j], u1[slot, pl.ds(j * depth, depth), cols],
+                                 preferred_element_type=F32)
+            part[c, :, cols] = total
+            return carry
+
+        lax.fori_loop(0, mc // 256, tile, 0)
+        hand_on(c, 0)
+
+    def restore(c):
+        slot = lax.rem(c, 2)
+        load(c, u2, u2_sem).wait()
+        doubled(c, 0).wait_recv()
+
+        def block(j, carry):
+            n = pl.ds(pl.multiple_of(j * depth, 16), depth)
+            rest[j] += lax.dot_general(filt[c], u2[slot, n, :], NT, preferred_element_type=F32)
+            return carry
+
+        lax.fori_loop(0, 4, block, 0)
+
+    def step(s, carry):
+        stage(s, 5, gathered)
+        stage(s, 4, gather)
+        stage(s, 3, scale)
+        stage(s, 2, add(1))
+        stage(s, 1, add(0))
+        stage(s, 0, rotate)
+        stage(s, LAG - 1, lambda c: load(c, u2, u2_sem).start())
+        stage(s, LAG, restore)
+        return carry
+
+    lax.fori_loop(0, CHUNKS + LAG, step, 0)
+
+    def across(k):
+        return copy(rest.at[2 * k + 1 - core], core_in.at[k], r_send.at[k], r_recv.at[k],
+                    row, core_peer)
+
+    for k in range(2):
+        across(k).start()
+
+    def reach_y():
+        return copy(y_out, y_in, r_send.at[2], r_recv.at[2], row, y_peer)
+
+    for k in range(2):
+        across(k).wait_recv()
+    y_out[...] = (rest[2 * (1 - y) + core] + core_in[1 - y]).astype(BF16)
+    reach_y().start()
+    for d in range(1, 8):
+        act_arrival(d).wait_recv()
+    own_a.wait()
+    kept = rest[col] + core_in[y]
+    reach_y().wait_recv()
+    restored = (kept + y_in[...].astype(F32)).astype(BF16)
+    for t in range(8):
+        place = (t % 2) * 4 + (t // 2 % 2) * 2 + t // 4
+        scores = lax.dot_general(restored, acts[t], NT, preferred_element_type=F32)
+        for q in range(4):
+            tot[q, place] = scores[q * 64:(q + 1) * 64]
+
+    def total_core(k):
+        return copy(tot.at[2 * k + 1 - core], tot_core.at[k], t_send.at[k], t_recv.at[k],
+                    row, core_peer)
+
+    total_core(1 - y).start()
+    total_core(y).start()
+    total_core(1 - y).wait_recv()
+    total_core(y).wait_recv()
+    tot[2 * (1 - y) + core] += tot_core[1 - y]
+    total_y = copy(tot.at[2 * (1 - y) + core], tot_y, t_send.at[2], t_recv.at[2], row, y_peer)
+    total_y.start()
+    tot[col] += tot_core[y]
+    total_y.wait_recv()
+    tot[col] += tot_y[...]
+
+    at = 0
+    row_sends = []
+    for k, (size, bit) in enumerate(((4, b0), (2, b1), (1, b2))):
+        mine, other = at + size * bit, at + size * (1 - bit)
+        landing = tot_row.at[pl.ds((0, 4, 6)[k], size)]
+        move = copy(tot.at[col, pl.ds(other, size)], landing, t_send.at[3 + k], t_recv.at[3 + k],
+                    peers[k], col)
+        move.start()
+        row_sends.append(move)
+        move.wait_recv()
+        if size > 1:
+            tot[col, pl.ds(mine, size)] += landing[...]
+        else:
+            out_ref[...] = tot[col, mine] + tot_row[6]
+        at = mine
+
+    own_y.wait_send()
+    own_c.wait_send()
+    fwd.wait_send()
+    for d in range(1, 8):
+        act_copy(d).wait_send()
+
+    def drain(c, carry):
+        for k in range(3):
+            halving(c, k).wait_send()
+            doubling(c, k).wait_send()
+        return carry
+
+    lax.fori_loop(0, CHUNKS, drain, 0)
+    for k in range(2):
+        across(k).wait_send()
+        total_core(k).wait_send()
+    reach_y().wait_send()
+    total_y.wait_send()
+    for move in row_sends:
+        move.wait_send()
+
+
+def fused(query_grads, eigenbasis, eigenvalues, activations):
+    depth, queries = query_grads.shape
+    n, m = eigenbasis.shape
+    mc = m // CHUNKS
+    tokens = activations.shape[0]
+    weights = filter_weights(eigenvalues).reshape(CHUNKS, 1, mc)
+    dma = pltpu.SemaphoreType.DMA
+    vmem = pl.BlockSpec(memory_space=pltpu.VMEM)
+    hbm = pl.BlockSpec(memory_space=pl.ANY)
+    return pl.pallas_call(
+        kernel,
+        out_shape=jax.ShapeDtypeStruct((queries // 4, tokens), F32),
+        in_specs=[vmem, hbm, vmem, hbm],
+        out_specs=vmem,
+        scratch_shapes=[
+            pltpu.VMEM((4, queries, depth), BF16),
+            pltpu.VMEM((2, n, mc), BF16),
+            pltpu.VMEM((2, n, mc), BF16),
+            pltpu.VMEM((CHUNKS, queries, mc), F32),
+            pltpu.VMEM((CHUNKS, 224, mc), BF16),
+            pltpu.VMEM((CHUNKS, 224, mc), BF16),
+            pltpu.VMEM((CHUNKS, queries, mc), BF16),
+            pltpu.VMEM((4, queries, depth), F32),
+            pltpu.VMEM((2, queries, depth), F32),
+            pltpu.VMEM((queries, depth), BF16),
+            pltpu.VMEM((queries, depth), BF16),
+            pltpu.VMEM((8, tokens, depth), BF16),
+            pltpu.VMEM((4, 8, queries // 4, tokens), F32),
+            pltpu.VMEM((2, 8, queries // 4, tokens), F32),
+            pltpu.VMEM((8, queries // 4, tokens), F32),
+            pltpu.VMEM((7, queries // 4, tokens), F32),
+            dma((2,)), dma((2,)),
+            dma((3,)), dma((3,)),
+            dma((8,)), dma((8,)), dma,
+            dma((6, CHUNKS)), dma((6, CHUNKS)),
+            dma((3,)), dma((3,)),
+            dma((6,)), dma((6,)),
+        ],
+        compiler_params=pltpu.CompilerParams(
+            collective_id=0, has_side_effects=True, vmem_limit_bytes=60 * 2**20
+        ),
+        cost_estimate=pl.CostEstimate(
+            flops=4 * n * m * queries, bytes_accessed=4 * n * m, transcendentals=0
+        ),
+    )(query_grads.T, eigenbasis, weights, activations.transpose(1, 0, 2))
+
+
+def general(query_grads, eigenbasis, eigenvalues, activations):
     grad_block = lax.all_gather(query_grads, "col", axis=0, tiled=True)
     share = eigenbasis.shape[1] // lax.axis_size("row")
     partial_rot = lax.psum_scatter(
@@ -38,6 +333,18 @@
     )
 
 
+def local(query_grads, eigenbasis, eigenvalues, activations):
+    sizes = (lax.axis_size("row"), lax.axis_size("col"))
+    fits = (
+        sizes == (8, 4)
+        and query_grads.shape[1] == 256
+        and eigenbasis.shape[1] % (256 * CHUNKS) == 0
+        and eigenbasis.shape[0] % 64 == 0
+        and activations.shape[0] == 128
+    )
+    return (fused if fits else general)(query_grads, eigenbasis, eigenvalues, activations)
+
+
 def solution(mesh):
     in_specs = (P(("row", "col"), None), P("row", "col"), P("col"), P("row", None, "col"))
     out_specs = P("col", "row")

time: 416 us -> 177 us (0.43)
  waiting for transfers between devices: 341 us -> 0 us
  Pallas kernels: 0 us -> 168 us
  matrix products: 50.6 us -> 0 us
  between operations: 13.5 us -> 0.01 us
    reduce_scatter x3 -> x0, waiting for transfers between devices: 186 us -> none  [the longest x1 128 us: local(): lax.psum_scatter(lax.dot_general(eigenbasis, grad_block, (((0,), (0,)), (...]
    pallas_call x0 -> x1, Pallas kernels: none -> 168 us  [fused(): pl.pallas_call(kernel, out_shape=jax.ShapeDtypeStruct((queries // 4, toke...]
    all_gather x3 -> x0, waiting for transfers between devices: 155 us -> none  [the longest x1 65.3 us: local(): blocks = lax.all_gather(restored, 'row', axis=0, tiled=True)]
    dot_general x3 -> x0, matrix products: 50.6 us -> none  [the longest x1 23.8 us: local(): lax.dot_general(eigenbasis, grad_block, (((0,), (0,)), ((), ())), preferr...]
  transfers between devices with their start and end apart: 6 -> 0, of which waited for: 6 -> 0; matrix products, arithmetic and copies ran while one was open for 0% -> 0% of each run, Pallas kernels for 0% -> 0%
where the time goes in v1:
time: 177 us; the launch traced here: 176 us
  Pallas kernels  168 us (95%)
  local copies, waits for them, and re-layouts  7.77 us (4%)
    pallas_call x1, Pallas kernels, fused(): pl.pallas_call(kernel, out_shape=jax.ShapeDtypeStruct((queries // 4, toke...  168 us
    unnamed x3, local copies, waits for them, and re-layouts  7.14 us

profile of v1, /device:TPU:0, one launch (start us, length us, event | category | flops | bytes accessed | tf_op | source)
XLA Modules:
  0.0 176.3 jit_solution(6348665195961265395)
XLA Ops:
  0.0 0.8 subtract_divide_fusion
  0.8 0.6 reshape.3.w_ref
  1.4 2.0 %copy.5 = bf16[864,256]{0,1:T(8,128)(2,1)} copy(bf16[864,256]{1,0:T(8,128)(2,1)} %param.4) | data formatting | bytes 884736 | tf_op args[0]
  3.4 3.8 %copy.6 = bf16[128,8,864]{2,0,1:T(8,128)(2,1)} copy(bf16[128,8,864]{0,2,1:T(8,128)(2,1)} %param.7) | data formatting | bytes 3538944 | tf_op args[3]
  7.2 167.7 %shard_map.46 = f32[64,128]{1,0:T(8,128)} custom-call(bf16[256,864]{1,0:T(8,128)(2,1)} %bitcast.3, bf16[3456,6912]{1,0:T(8,128)(2,1)} %u_ref.1, f32[9,1,768]{2,1,0:T(1,128)} %reshape.3.w_ref, bf16[8,128,864]{2,1,0:T(8,128)(2,1)} %bitcast.2), custom_call_target="tpu_custom_call" | custom-call | flops 24461180928 | bytes 95551488 | tf_op jit(solution)/shard_map/pallas_call | solution.py:268
  174.9 1.4 copy.8

commit v2 on v1

--- a/solution.py
+++ b/solution.py
@@ -9,6 +9,7 @@
 
 CHUNKS = 9
 LAG = 6
+SPREAD = 4
 F32, BF16 = jnp.float32, jnp.bfloat16
 NT = (((1,), (1,)), ((), ()))
 
@@ -20,9 +21,9 @@
 def kernel(
     gt_ref, u_ref, w_ref, act_ref, out_ref,
     gt, u1, u2, part, send, recv, filt, rest, core_in, y_out, y_in,
-    acts, tot, tot_core, tot_y, tot_row,
+    acts, tot, tot_row,
     u1_sem, u2_sem, g_send, g_recv, a_send, a_recv, a_own, x_send, x_recv,
-    r_send, r_recv, t_send, t_recv,
+    r_send, r_recv, t_send, t_recv, s_send, s_recv,
 ):
     row, col = lax.axis_index("row"), lax.axis_index("col")
     b0, b1, b2 = lax.rem(row, 2), lax.rem(lax.div(row, 2), 2), lax.div(row, 4)
@@ -60,16 +61,36 @@
     own_c.start()
     gt[col] = gt_ref[...]
 
-    own_a = pltpu.make_async_copy(act_ref.at[row], acts.at[row], a_own)
+    own_a = pltpu.make_async_copy(act_ref.at[row], acts.at[col, row], a_own)
     own_a.start()
 
     def act_copy(d):
         to = lax.rem(row + d, 8)
-        return copy(act_ref.at[to], acts.at[row], a_send.at[d], a_recv.at[d], to, col)
+        return copy(act_ref.at[to], acts.at[col, row], a_send.at[d], a_recv.at[d], to, col)
 
     def act_arrival(d):
         origin = lax.rem(row + 8 - d, 8)
-        return copy(act_ref.at[row], acts.at[origin], a_send.at[d], a_recv.at[d], origin, col)
+        return copy(act_ref.at[row], acts.at[col, origin], a_send.at[d], a_recv.at[d], origin, col)
+
+    def block_of(c, d):
+        return acts.at[c, lax.rem(row + 8 - d, 8)]
+
+    def over_y(c, d):
+        return copy(block_of(c, d), block_of(c, d), s_send.at[0, d], s_recv.at[0, d], row, y_peer)
+
+    def over_core(c, d, k):
+        return copy(block_of(c, d), block_of(c, d), s_send.at[k, d], s_recv.at[k, d],
+                    row, core_peer)
+
+    def spread(d):
+        pl.when(d == 0)(lambda: own_a.wait())
+        pl.when(d > 0)(lambda: act_arrival(d).wait_recv())
+        over_y(col, d).start()
+        over_core(col, d, 1).start()
+
+    def relay(d):
+        over_y(y_peer, d).wait_recv()
+        over_core(y_peer, d, 2).start()
 
     for d in range(1, 8):
         act_copy(d).start()
@@ -165,73 +186,69 @@
         lax.fori_loop(0, 4, block, 0)
 
     def step(s, carry):
+        stage(s, LAG - 1, lambda c: load(c, u2, u2_sem).start())
+        stage(s, 0, rotate)
         stage(s, 5, gathered)
         stage(s, 4, gather)
         stage(s, 3, scale)
         stage(s, 2, add(1))
         stage(s, 1, add(0))
-        stage(s, 0, rotate)
-        stage(s, LAG - 1, lambda c: load(c, u2, u2_sem).start())
+        pl.when(jnp.logical_and(s >= SPREAD, s < SPREAD + 8))(lambda: spread(s - SPREAD))
+        pl.when(jnp.logical_and(s >= SPREAD + 2, s < SPREAD + 10))(lambda: relay(s - SPREAD - 2))
         stage(s, LAG, restore)
         return carry
 
     lax.fori_loop(0, CHUNKS + LAG, step, 0)
 
+    queries = out_ref.shape[0]
+
+    def part_of(j):
+        return pl.ds(pl.multiple_of(j * queries, queries), queries)
+
     def across(k):
-        return copy(rest.at[2 * k + 1 - core], core_in.at[k], r_send.at[k], r_recv.at[k],
-                    row, core_peer)
-
-    for k in range(2):
-        across(k).start()
+        return copy(rest.at[:, part_of(2 * k + 1 - core)], core_in.at[k], r_send.at[k],
+                    r_recv.at[k], row, core_peer)
+
+    across(1 - y).start()
+    across(y).start()
 
     def reach_y():
         return copy(y_out, y_in, r_send.at[2], r_recv.at[2], row, y_peer)
 
-    for k in range(2):
-        across(k).wait_recv()
-    y_out[...] = (rest[2 * (1 - y) + core] + core_in[1 - y]).astype(BF16)
+    across(1 - y).wait_recv()
+    y_out[...] = (rest[:, part_of(2 * (1 - y) + core)] + core_in[1 - y]).astype(BF16)
     reach_y().start()
-    for d in range(1, 8):
-        act_arrival(d).wait_recv()
-    own_a.wait()
-    kept = rest[col] + core_in[y]
+    across(y).wait_recv()
+    core_in[y] += rest[:, part_of(col)]
+    for d in range(8):
+        over_core(core_peer, d, 1).wait_recv()
+        over_core(diagonal, d, 2).wait_recv()
     reach_y().wait_recv()
-    restored = (kept + y_in[...].astype(F32)).astype(BF16)
+    restored = core_in[y] + y_in[...].astype(F32)
+    high = restored.astype(BF16)
+    low = (restored - high.astype(F32)).astype(BF16)
+    both = jnp.concatenate([high, low], axis=1)
     for t in range(8):
         place = (t % 2) * 4 + (t // 2 % 2) * 2 + t // 4
-        scores = lax.dot_general(restored, acts[t], NT, preferred_element_type=F32)
-        for q in range(4):
-            tot[q, place] = scores[q * 64:(q + 1) * 64]
-
-    def total_core(k):
-        return copy(tot.at[2 * k + 1 - core], tot_core.at[k], t_send.at[k], t_recv.at[k],
-                    row, core_peer)
-
-    total_core(1 - y).start()
-    total_core(y).start()
-    total_core(1 - y).wait_recv()
-    total_core(y).wait_recv()
-    tot[2 * (1 - y) + core] += tot_core[1 - y]
-    total_y = copy(tot.at[2 * (1 - y) + core], tot_y, t_send.at[2], t_recv.at[2], row, y_peer)
-    total_y.start()
-    tot[col] += tot_core[y]
-    total_y.wait_recv()
-    tot[col] += tot_y[...]
+        scores = jnp.zeros((2 * queries, acts.shape[2]), F32)
+        for j in range(4):
+            scores += lax.dot_general(both[j], acts[j, t], NT, preferred_element_type=F32)
+        tot[place] = scores[:queries] + scores[queries:]
 
     at = 0
     row_sends = []
     for k, (size, bit) in enumerate(((4, b0), (2, b1), (1, b2))):
         mine, other = at + size * bit, at + size * (1 - bit)
         landing = tot_row.at[pl.ds((0, 4, 6)[k], size)]
-        move = copy(tot.at[col, pl.ds(other, size)], landing, t_send.at[3 + k], t_recv.at[3 + k],
+        move = copy(tot.at[pl.ds(other, size)], landing, t_send.at[k], t_recv.at[k],
                     peers[k], col)
         move.start()
         row_sends.append(move)
         move.wait_recv()
         if size > 1:
-            tot[col, pl.ds(mine, size)] += landing[...]
+            tot[pl.ds(mine, size)] += landing[...]
         else:
-            out_ref[...] = tot[col, mine] + tot_row[6]
+            out_ref[...] = tot[mine] + tot_row[6]
         at = mine
 
     own_y.wait_send()
@@ -249,9 +266,11 @@
     lax.fori_loop(0, CHUNKS, drain, 0)
     for k in range(2):
         across(k).wait_send()
-        total_core(k).wait_send()
     reach_y().wait_send()
-    total_y.wait_send()
+    for d in range(8):
+        over_y(col, d).wait_send()
+        over_core(col, d, 1).wait_send()
+        over_core(y_peer, d, 2).wait_send()
     for move in row_sends:
         move.wait_send()
 
@@ -279,12 +298,10 @@
             pltpu.VMEM((CHUNKS, 224, mc), BF16),
             pltpu.VMEM((CHUNKS, queries, mc), BF16),
             pltpu.VMEM((4, queries, depth), F32),
-            pltpu.VMEM((2, queries, depth), F32),
-            pltpu.VMEM((queries, depth), BF16),
-            pltpu.VMEM((queries, depth), BF16),
-            pltpu.VMEM((8, tokens, depth), BF16),
-            pltpu.VMEM((4, 8, queries // 4, tokens), F32),
-            pltpu.VMEM((2, 8, queries // 4, tokens), F32),
+            pltpu.VMEM((2, 4, queries // 4, depth), F32),
+            pltpu.VMEM((4, queries // 4, depth), BF16),
+            pltpu.VMEM((4, queries // 4, depth), BF16),
+            pltpu.VMEM((4, 8, tokens, depth), BF16),
             pltpu.VMEM((8, queries // 4, tokens), F32),
             pltpu.VMEM((7, queries // 4, tokens), F32),
             dma((2,)), dma((2,)),
@@ -292,7 +309,8 @@
             dma((8,)), dma((8,)), dma,
             dma((6, CHUNKS)), dma((6, CHUNKS)),
             dma((3,)), dma((3,)),
-            dma((6,)), dma((6,)),
+            dma((3,)), dma((3,)),
+            dma((3, 8)), dma((3, 8)),
         ],
         compiler_params=pltpu.CompilerParams(
             collective_id=0, has_side_effects=True, vmem_limit_bytes=60 * 2**20

time: 177 us -> 160 us (0.904)
  Pallas kernels: 168 us -> 151 us
    pallas_call x1, Pallas kernels: 168 us -> 151 us  [fused(): pl.pallas_call(kernel, out_shape=jax.ShapeDtypeStruct((queries // 4, toke...]
where the time goes in v2:
time: 160 us; the launch traced here: 159 us
  Pallas kernels  151 us (94%)
  local copies, waits for them, and re-layouts  7.77 us (5%)
    pallas_call x1, Pallas kernels, fused(): pl.pallas_call(kernel, out_shape=jax.ShapeDtypeStruct((queries // 4, toke...  151 us
    unnamed x3, local copies, waits for them, and re-layouts  7.14 us

profile of v2, /device:TPU:0, one launch (start us, length us, event | category | flops | bytes accessed | tf_op | source)
XLA Modules:
  0.0 159.3 jit_solution(9695400995252701860)
XLA Ops:
  0.0 0.8 subtract_divide_fusion
  0.8 0.6 reshape.3.w_ref
  1.4 2.0 %copy.5 = bf16[864,256]{0,1:T(8,128)(2,1)} copy(bf16[864,256]{1,0:T(8,128)(2,1)} %param.4) | data formatting | bytes 884736 | tf_op args[0]
  3.4 3.8 %copy.6 = bf16[128,8,864]{2,0,1:T(8,128)(2,1)} copy(bf16[128,8,864]{0,2,1:T(8,128)(2,1)} %param.7) | data formatting | bytes 3538944 | tf_op args[3]
  7.2 150.7 %shard_map.46 = f32[64,128]{1,0:T(8,128)} custom-call(bf16[256,864]{1,0:T(8,128)(2,1)} %bitcast.3, bf16[3456,6912]{1,0:T(8,128)(2,1)} %u_ref.1, f32[9,1,768]{2,1,0:T(1,128)} %reshape.3.w_ref, bf16[8,128,864]{2,1,0:T(8,128)(2,1)} %bitcast.2), custom_call_target="tpu_custom_call" | custom-call | flops 24461180928 | bytes 95551488 | tf_op jit(solution)/shard_map/pallas_call | solution.py:287
  157.9 1.4 copy.8
